TPU v7x, 128 devices: a whole 4x4x4 slice. The times are simulated.
128 devices in a mesh: ctx: 16 (over y_lo, z, core), head: 8 (over x, y_hi).
Axes of the slice: x: 4, y: 4 (y_hi: 2, y_lo: 2; y = y_hi * 2 + y_lo), z: 4, core: 2. Of those that a mesh axis runs over, the one named last changes fastest.
Arguments:
- queries: bfloat16 [2048, 36864], P('ctx', 'head'), may hold values from -296 to 296
- latent_keys: bfloat16 [2048, 576], P('ctx'), may hold values from -9 to 9
- block_order: int32 [16], replicated, may hold values from 0 to 15, each once
- out_grad: bfloat16 [2048, 32768], P('ctx', 'head'), may hold values from -6 to 6
Outputs:
- attended: bfloat16 [2048, 32768], P('ctx', 'head')
- query_grad: bfloat16 [2048, 36864], P('ctx', 'head')
- latent_grad: bfloat16 [2048, 576], P('ctx')
Inputs may be any that keep to these rules, and one draw needn't show every extreme that they name: `block_order`: a permutation: each block index once.
All inputs are finite; a program needn't handle non-finite values.
Results may differ from a plain program's by a relative error of at most 0.034.
Values may be sent and summed in bfloat16 or wider, within the bound.
A program may use at most 64 MiB of HBM per device.

v0:
```python
import jax
import jax.numpy as jnp
from jax import lax
from jax.sharding import PartitionSpec as P

LATENT = 512
ROPE = 64
score_scale = 192.0 ** (-0.5)
masked_value = -1e30


def row_positions(block_order, first_row, count, shard_rows):
    rows = first_row + jnp.arange(count, dtype=jnp.int32)
    owner = rows // shard_rows
    blocks = block_order.shape[0]
    onehot = (owner[:, None] == jnp.arange(blocks, dtype=jnp.int32)[None, :]).astype(jnp.int32)
    base = jnp.sum(onehot * block_order[None, :], axis=1)
    return base * shard_rows + rows % shard_rows


def local(queries, latent_keys, block_order, out_grad):
    kdim = LATENT + ROPE
    shard_rows = latent_keys.shape[0]
    head_count = queries.shape[1] // kdim
    query_three = queries.reshape(shard_rows, head_count, kdim)
    grad_three = out_grad.reshape(shard_rows, head_count, LATENT)
    own_index = lax.axis_index("ctx")
    query_pos = row_positions(block_order, own_index * shard_rows, shard_rows, shard_rows)

    def piece_scores(piece, start):
        score = (
            jnp.einsum("thd,pd->htp", query_three, piece, preferred_element_type=jnp.float32)
            * score_scale
        )
        key_pos = row_positions(block_order, start, piece.shape[0], shard_rows)
        visible = key_pos[None, :] <= query_pos[:, None]
        return (jnp.where(visible[None], score, masked_value), visible)

    running_max = jnp.full((head_count, shard_rows), masked_value, jnp.float32)
    score, visible = piece_scores(
        lax.all_gather(latent_keys, "ctx", axis=0, tiled=True), jnp.int32(0)
    )
    new_max = jnp.maximum(running_max, jnp.max(score, axis=2))
    weights = jnp.where(visible[None], jnp.exp(score - new_max[:, :, None]), 0.0)
    new_sum = jnp.sum(weights, axis=2)
    lse = new_max + jnp.log(new_sum)
    piece = lax.all_gather(latent_keys, "ctx", axis=0, tiled=True)
    score, visible = piece_scores(piece, jnp.int32(0))
    prob_b = jnp.where(visible[None], jnp.exp(score - lse[:, :, None]), 0.0).astype(jnp.bfloat16)
    accum = jnp.einsum("htp,pe->the", prob_b, piece[:, :LATENT], preferred_element_type=jnp.float32)
    attended = accum.astype(jnp.bfloat16)
    delta = jnp.sum(attended.astype(jnp.float32) * grad_three.astype(jnp.float32), axis=2).T
    piece = lax.all_gather(latent_keys, "ctx", axis=0, tiled=True)
    score, visible = piece_scores(piece, jnp.int32(0))
    prob = jnp.where(visible[None], jnp.exp(score - lse[:, :, None]), 0.0)
    prob_b = prob.astype(jnp.bfloat16)
    dprob = jnp.einsum(
        "the,pe->htp", grad_three, piece[:, :LATENT], preferred_element_type=jnp.float32
    )
    dscore = (prob * (dprob - delta[:, :, None])).astype(jnp.bfloat16)
    query_accum = jnp.einsum("htp,pd->thd", dscore, piece, preferred_element_type=jnp.float32)
    key_part = score_scale * jnp.einsum(
        "htp,thd->pd", dscore, query_three, preferred_element_type=jnp.float32
    )
    value_part = jnp.einsum("htp,the->pe", prob_b, grad_three, preferred_element_type=jnp.float32)
    term = key_part + jnp.pad(value_part, ((0, 0), (0, ROPE)))
    key_accum = term
    query_accum, key_accum = (query_accum, key_accum)
    query_grad = (
        (score_scale * query_accum).astype(jnp.bfloat16).reshape(shard_rows, head_count * kdim)
    )
    partial_rows = lax.psum_scatter(key_accum, "ctx", scatter_dimension=0, tiled=True)
    latent_grad = lax.psum(partial_rows, "head").astype(jnp.bfloat16)
    return (attended.reshape(shard_rows, head_count * LATENT), query_grad, latent_grad)


def solution(mesh):
    placed = (P("ctx", "head"), P("ctx", None), P(), P("ctx", "head"))
    return jax.shard_map(
        local,
        mesh=mesh,
        in_specs=placed,
        out_specs=(P("ctx", "head"), P("ctx", "head"), P("ctx", None)),
        check_vma=False,
    )
```

profile of v0, /device:TPU:0, one launch (start us, length us, event | category | flops | bytes accessed | tf_op | source)
XLA Modules:
  0.0 196.5 jit_solution(11976603212448171671)
XLA Ops:
  7.2 0.0 copy-start
  7.2 0.0 copy-start.3
  7.2 0.0 all-gather.2.cloned.1.call-start
  7.2 0.7 all-gather.2.cloned.1.call-update
  7.9 0.0 reduce-scatter.2.cloned.1.call-start
  8.0 1.6 copy.34
  9.6 1.3 copy.37
  10.9 0.0 copy-done
  10.9 0.7 copy.30
  11.7 0.0 copy-done.3
  11.7 0.1 select_reduce_fusion.2
  11.8 0.1 select_reduce_fusion.1
  11.9 0.3 broadcast_compare_fusion
  12.2 38.2 %all-gather.2.cloned.1.call-done = bf16[2048,576]{0,1:T(8,128)(2,1)} async-done(((bf16[128,576]{0,1:T(8,128)(2,1)}), bf16[2048,576]{0,1:T(8,128)(2,1)}) %all-gather.2.cloned.1.call-update) | async-done | bytes 2359312 | tf_op jit(solution)/shard_map/all_gather | solution.py:47
  50.5 5.6 %fusion.3 = (f32[8,128]{1,0:T(8,128)S(1)}, f32[2048,128,8]{1,0,2:T(8,128)S(1)}) fusion(pred[128,2048]{0,1:T(8,128)(4,1)S(1)} %broadcast_compare_fusion, bf16[128,8,576]{0,2,1:T(8,128)(2,1)S(1)} %bitcast.65, bf16[2048,576]{0,1:T(8,128)(2,1)} %all-gather.2.cloned.1.call-done), kind=kOutput, calls=%fused_computation.7 | convolution fusion | flops 2422209536 | bytes 12193792 | tf_op jit(solution)/shard_map/thd,pd->htp/dot_general | solution.py:32
  56.1 2.0 %select_reduce_fusion = f32[8,128]{1,0:T(8,128)S(1)} fusion(f32[2048,128,8]{1,0,2:T(8,128)S(1)} %get-tuple-element.13, f32[8,128]{1,0:T(8,128)S(1)} %broadcast_maximum_fusion, pred[128,2048]{0,1:T(8,128)(4,1)S(1)} %broadcast_compare_fusion), kind=kLoop, calls=%fused_computation.5 | loop fusion | flops 10484736 | bytes 8658944 | tf_op jit(solution)/shard_map/reduce_sum | solution.py:45
  58.1 0.0 copy-start.1
  58.2 0.0 copy-start.4
  58.2 2.7 %convolution_bitcast_fusion = f32[2048,512]{0,1:T(8,128)S(1)} fusion(bf16[128,8,512]{0,2,1:T(8,128)(2,1)S(1)} %bitcast.62, f32[2048,128,8]{1,0,2:T(8,128)S(1)} %get-tuple-element.13, f32[8,128]{1,0:T(8,128)S(1)} %log_add_fusion, pred[128,2048]{0,1:T(8,128)(4,1)S(1)} %broadcast_compare_fusion), kind=kOutput, calls=%fused_computation.10 | convolution fusion | flops 2157969408 | bytes 13897728 | tf_op jit(solution)/shard_map/htp,the->pe/dot_general | solution.py:65
  60.9 0.0 copy-done.1
  60.9 3.7 %multiply_reduce_fusion = (f32[128,8]{0,1:T(8,128)S(1)}, bf16[128,8,512]{2,0,1:T(8,128)(2,1)}) fusion(bf16[128,8,512]{2,0,1:T(8,128)(2,1)S(1)} %copy-done.1, bf16[2048,576]{0,1:T(8,128)(2,1)S(1)} %copy-done.4, f32[2048,128,8]{1,0,2:T(8,128)S(1)} %get-tuple-element.13, f32[8,128]{1,0:T(8,128)S(1)} %log_add_fusion, ...), kind=kOutput, calls=%fused_computation.17 | convolution fusion | flops 2160589824 | bytes 12853248 | tf_op jit(solution)/shard_map/htp,pe->the/dot_general | solution.py:50
  64.6 4.5 %fusion.1 = bf16[8,128,2048]{1,2,0:T(8,128)(2,1)S(1)} fusion(f32[2048,128,8]{1,0,2:T(8,128)S(1)} %get-tuple-element.13, bf16[128,8,512]{0,2,1:T(8,128)(2,1)S(1)} %bitcast.63, f32[8,128]{1,0:T(8,128)S(1)} %bitcast.68, f32[8,128]{1,0:T(8,128)S(1)} %log_add_fusion, pred[128,2048]{0,1:T(8,128)(4,1)S(1)} %broadcast_compare_fusion, bf16[2048,576]{0,1:T(8,128)(2,1)S(1)} %copy-done.4), kind=kOutput, calls=%fused_computation.2 | convolution fusion | flops 2162163712 | bytes 15998976 | tf_op jit(solution)/shard_map/the,pe->htp/dot_general | solution.py:57
  69.0 2.0 %copy-done.5 = bf16[8,128,2048]{1,2,0:T(8,128)(2,1)} copy-done((bf16[8,128,2048]{1,2,0:T(8,128)(2,1)}, bf16[8,128,2048]{1,2,0:T(8,128)(2,1)S(1)}, u32[]{:S(2)}) %copy-start.5) | copy-done | bytes 4194328
  71.0 4.3 %fusion.4 = f32[2048,576]{0,1:T(8,128)} fusion(f32[2048,512]{0,1:T(8,128)S(1)} %convolution_bitcast_fusion, bf16[8,128,2048]{1,2,0:T(8,128)(2,1)S(1)} %fusion.1, bf16[128,8,576]{0,2,1:T(8,128)(2,1)S(1)} %bitcast.66), kind=kOutput, calls=%fused_computation.9 | convolution fusion | flops 2418278400 | bytes 14286848 | tf_op jit(solution)/shard_map/htp,thd->pd/dot_general | solution.py:62
  75.4 0.0 reduce-scatter.2.cloned.1.call-update
  75.4 1.2 copy-done.2
  76.6 0.7 copy.33
  77.2 1.3 copy.41
  78.6 5.5 %multiply_convert_fusion = bf16[8,128,576]{1,2,0:T(8,128)(2,1)S(1)} fusion(bf16[8,128,2048]{1,2,0:T(8,128)(2,1)} %copy-done.5, bf16[2048,576]{0,1:T(8,128)(2,1)} %all-gather.2.cloned.1.call-done), kind=kOutput, calls=%fused_computation.15 | convolution fusion | flops 2417098752 | bytes 7733248 | tf_op jit(solution)/shard_map/htp,pd->thd/dot_general | solution.py:61
  84.1 1.4 copy.42
  85.5 58.2 %reduce-scatter.2.cloned.1.call-done = f32[128,576]{0,1:T(8,128)} async-done(((f32[2048,576]{0,1:T(8,128)}), f32[128,576]{0,1:T(8,128)}) %reduce-scatter.2.cloned.1.call-update) | async-done | bytes 294928 | tf_op jit(solution)/shard_map/reduce_scatter | solution.py:72
  143.7 45.9 %all-reduce.2 = bf16[128,576]{0,1:T(8,128)(2,1)} all-reduce(f32[128,576]{0,1:T(8,128)} %reduce-scatter.2.cloned.1.call-done), channel_id=1, replica_groups=mesh['ctx'=16,'head'=8] {'head'}, use_global_device_ids=true, to_apply=%region_6.7 | all-reduce | flops 73728 | bytes 442368 | tf_op jit(solution)/shard_map/psum | solution.py:73
  (9 shorter events, 0.1 us)
Async XLA Ops:
  7.2 3.7 %copy-start = (bf16[128,4608]{1,0:T(8,128)(2,1)S(1)}, bf16[128,4608]{1,0:T(8,128)(2,1)}, u32[]{:S(2)}) copy-start(bf16[128,4608]{1,0:T(8,128)(2,1)} %param.4) | copy-start | bytes 3538948
  7.2 4.5 %copy-start.3 = (s32[16]{0:T(128)S(1)}, s32[16]{0:T(128)}, u32[]{:S(2)}) copy-start(s32[16]{0:T(128)} %param.6) | copy-start | bytes 196
  7.2 43.3 %all-gather.2.cloned.1.call-start = ((), (), s32[]{:S(2)}) async-start(), calls=%async_computation.1 | async-start | bytes 2506752 | tf_op jit(solution)/shard_map/all_gather | solution.py:47
  7.9 135.8 %reduce-scatter.2.cloned.1.call-start = ((), (), s32[]{:S(2)}) async-start(), calls=%async_computation.2 | async-start | bytes 5013504 | tf_op jit(solution)/shard_map/reduce_scatter | solution.py:72
  58.1 2.7 %copy-start.1 = (bf16[128,8,512]{2,0,1:T(8,128)(2,1)S(1)}, bf16[128,8,512]{2,0,1:T(8,128)(2,1)}, u32[]{:S(2)}) copy-start(bf16[128,8,512]{2,0,1:T(8,128)(2,1)} %copy.37) | copy-start | bytes 3145732
  58.2 2.7 %copy-start.4 = (bf16[2048,576]{0,1:T(8,128)(2,1)S(1)}, bf16[2048,576]{0,1:T(8,128)(2,1)}, u32[]{:S(2)}) copy-start(bf16[2048,576]{0,1:T(8,128)(2,1)} %all-gather.2.cloned.1.call-done) | copy-start | bytes 7077892
  69.0 2.0 %copy-start.5 = (bf16[8,128,2048]{1,2,0:T(8,128)(2,1)}, bf16[8,128,2048]{1,2,0:T(8,128)(2,1)S(1)}, u32[]{:S(2)}) copy-start(bf16[8,128,2048]{1,2,0:T(8,128)(2,1)S(1)} %fusion.1) | copy-start | bytes 12582916
  75.4 1.2 copy-start.2
Sparse Core Ops, SparseCore 0:
  9.6 40.7 all-gather.1
  75.5 68.1 reduce-scatter.1
where the time goes:
time: 197 us; the launch traced here: 196 us
  waiting for transfers between devices  97.2 us (49%)
  blocking collectives  45.9 us (23%)
  matrix products  26.2 us (13%)
  between operations  14.2 us (7%)
  local copies, waits for them, and re-layouts  10.3 us (5%)
  other arithmetic  2.6 us (1%)
    reduce_scatter x1, waiting for transfers between devices, local(): lax.psum_scatter(key_accum, 'ctx', scatter_dimension=0, tiled=True)  58.2 us
    psum x1, blocking collectives, local(): latent_grad = lax.psum(partial_rows, 'head').astype(jnp.bfloat16)  45.9 us
    all_gather x1, waiting for transfers between devices, local(): piece = lax.all_gather(latent_keys, 'ctx', axis=0, tiled=True)  38.2 us
    unnamed x16, local copies, waits for them, and re-layouts  8.29 us
    dot_general x1, matrix products, piece_scores(): jnp.einsum('thd,pd->htp', query_three, piece, preferred_element_type=jnp....  5.59 us
    dot_general x1, matrix products, local(): jnp.einsum('htp,pd->thd', dscore, piece, preferred_element_type=jnp.float32)  5.5 us
    dot_general x1, matrix products, local(): jnp.einsum('the,pe->htp', grad_three, piece[:, :LATENT], preferred_elemen...  4.47 us
    dot_general x1, matrix products, local(): jnp.einsum('htp,thd->pd', dscore, query_three, preferred_element_type=jnp...  4.31 us
  transfers between devices with their start and end apart: 2, of which 2 were waited for; matrix products, arithmetic and copies ran while one was open for 7% of the time, Pallas kernels for 0%

commit v1 on v0

--- a/solution.py
+++ b/solution.py
@@ -1,3 +1,4 @@
+import functools
 import jax
 import jax.numpy as jnp
 from jax import lax
@@ -7,6 +8,17 @@
 ROPE = 64
 score_scale = 192.0 ** (-0.5)
 masked_value = -1e30
+
+
+def mark_the_clusters(u_in, axis_name):
+    z_new = lax.axis_size(axis_name)
+    local_part = jnp.stack(z_new * [u_in], axis=0)
+    carry_out = lax.all_to_all(local_part, axis_name, 0, 0)
+    arr_next = jnp.concatenate(carry_out, axis=0)
+    return arr_next
+
+
+choose_loops = functools.partial(mark_the_clusters, axis_name="ctx")
 
 
 def row_positions(block_order, first_row, count, shard_rows):
@@ -44,7 +56,7 @@
     weights = jnp.where(visible[None], jnp.exp(score - new_max[:, :, None]), 0.0)
     new_sum = jnp.sum(weights, axis=2)
     lse = new_max + jnp.log(new_sum)
-    piece = lax.all_gather(latent_keys, "ctx", axis=0, tiled=True)
+    piece = choose_loops(latent_keys)
     score, visible = piece_scores(piece, jnp.int32(0))
     prob_b = jnp.where(visible[None], jnp.exp(score - lse[:, :, None]), 0.0).astype(jnp.bfloat16)
     accum = jnp.einsum("htp,pe->the", prob_b, piece[:, :LATENT], preferred_element_type=jnp.float32)

time: 197 us -> 227 us (1.15)
  local copies, waits for them, and re-layouts: 10.3 us -> 25.5 us
  matrix products: 26.2 us -> 37.7 us
  starting transfers between devices: 0.08 us -> 6.59 us
  waiting for transfers between devices: 97.2 us -> 93.6 us
    all_gather x1, waiting for transfers between devices: 38.2 us -> 1.92 us  [local(): lax.all_gather(latent_keys, 'ctx', axis=0, tiled=True)]
    all_to_all x0 -> x1, waiting for transfers between devices: none -> 31.6 us  [mark_the_clusters(): carry_out = lax.all_to_all(local_part, axis_name, 0, 0)]
    reshape x0 -> x2, local copies, waits for them, and re-layouts: none -> 6.73 us  [mark_the_clusters(): arr_next = jnp.concatenate(carry_out, axis=0)]
    all_to_all x0 -> x1, starting transfers between devices: none -> 6.51 us  [mark_the_clusters(): carry_out = lax.all_to_all(local_part, axis_name, 0, 0)]
    dot_general x1, matrix products: 3.67 us -> 9.94 us  [local(): jnp.einsum('htp,pe->the', prob_b, piece[:, :LATENT], preferred_element_ty...]
    all_to_all x0 -> x1, local copies, waits for them, and re-layouts: none -> 2.94 us  [mark_the_clusters(): carry_out = lax.all_to_all(local_part, axis_name, 0, 0)]
    another operation x0 -> x1, local copies, waits for them, and re-layouts: none -> 2.79 us  [mark_the_clusters(): local_part = jnp.stack(z_new * [u_in], axis=0)]
    dot_general x1, matrix products: 4.47 us -> 7.25 us  [local(): jnp.einsum('the,pe->htp', grad_three, piece[:, :LATENT], preferred_elemen...]
  transfers between devices with their start and end apart: 2 -> 3, of which waited for: 2 -> 3; matrix products, arithmetic and copies ran while one was open for 7% -> 12% of each run, Pallas kernels for 0% -> 0%
where the time goes in v1:
time: 227 us
  waiting for transfers between devices  93.6 us (41%)
  blocking collectives  45.8 us (20%)
  matrix products  37.7 us (17%)
  local copies, waits for them, and re-layouts  25.5 us (11%)
  between operations  14.2 us (6%)
  starting transfers between devices  6.59 us (3%)
  other arithmetic  3.48 us (2%)
    reduce_scatter x1, waiting for transfers between devices, local(): lax.psum_scatter(key_accum, 'ctx', scatter_dimension=0, tiled=True)  59.4 us
    psum x1, blocking collectives, local(): latent_grad = lax.psum(partial_rows, 'head').astype(jnp.bfloat16)  45.8 us
    all_to_all x1, waiting for transfers between devices, mark_the_clusters(): carry_out = lax.all_to_all(local_part, axis_name, 0, 0)  31.6 us
    unnamed x20, local copies, waits for them, and re-layouts  11 us
    dot_general x1, matrix products, local(): jnp.einsum('htp,pe->the', prob_b, piece[:, :LATENT], preferred_element_ty...  9.94 us
    dot_general x1, matrix products, local(): jnp.einsum('the,pe->htp', grad_three, piece[:, :LATENT], preferred_elemen...  7.25 us
    reshape x2, local copies, waits for them, and re-layouts, mark_the_clusters(): arr_next = jnp.concatenate(carry_out, axis=0)  6.73 us
    all_to_all x1, starting transfers between devices, mark_the_clusters(): carry_out = lax.all_to_all(local_part, axis_name, 0, 0)  6.51 us
  transfers between devices with their start and end apart: 3, of which 3 were waited for; matrix products, arithmetic and copies ran while one was open for 12% of the time, Pallas kernels for 0%

profile of v1, /device:TPU:0, one launch (start us, length us, event | category | flops | bytes accessed | tf_op | source)
XLA Modules:
  0.0 226.9 jit_solution(17805520162609653825)
XLA Ops:
  7.2 0.0 all-gather.2.cloned.1.call-start
  7.2 0.7 all-gather.2.cloned.1.call-update
  7.9 2.8 %stack.2 = bf16[16,128,576]{1,2,0:T(8,128)(2,1)} broadcast(bf16[128,576]{0,1:T(8,128)(2,1)} %param.5), dimensions={1,2} | broadcast | bytes 2506752 | tf_op jit(solution)/shard_map/stack | solution.py:15
  10.7 6.5 %all-to-all-start = ((bf16[16,128,576]{1,2,0:T(8,128)(2,1)}), bf16[16,128,576]{1,2,0:T(8,128)(2,1)S(1)}, u32[]{:S(2)}, u32[]{:S(2)}) async-start(bf16[16,128,576]{1,2,0:T(8,128)(2,1)} %stack.2), calls=%async_computation | async-start | bytes 4718592 | tf_op jit(solution)/shard_map/all_to_all | solution.py:16
  17.2 0.0 reduce-scatter.2.cloned.1.call-start
  17.3 1.6 copy.49
  18.9 1.3 copy.52
  20.2 2.4 %copy.45 = bf16[128,4608]{0,1:T(8,128)(2,1)} copy(bf16[128,4608]{1,0:T(8,128)(2,1)} %param.4) | data formatting | bytes 2359296 | tf_op args[0]
  22.6 0.1 select_reduce_fusion.2
  22.7 0.1 select_reduce_fusion.1
  22.8 1.0 broadcast_compare_fusion
  23.9 31.6 %all-to-all-done = bf16[16,128,576]{1,2,0:T(8,128)(2,1)S(1)} async-done(((bf16[16,128,576]{1,2,0:T(8,128)(2,1)}), bf16[16,128,576]{1,2,0:T(8,128)(2,1)S(1)}, u32[]{:S(2)}, u32[]{:S(2)}) %all-to-all-start) | async-done | bytes 2359328 | tf_op jit(solution)/shard_map/all_to_all | solution.py:16
  55.5 2.9 %copy.44 = bf16[16,128,576]{1,0,2:T(8,128)(2,1)} copy(bf16[16,128,576]{1,2,0:T(8,128)(2,1)S(1)} %all-to-all-done) | data formatting | bytes 4718592 | tf_op jit(solution)/shard_map/all_to_all | solution.py:16
  58.5 5.0 %reshape.128 = bf16[2048,576,1]{0,1,2:T(8,128)(2,1)} reshape(bf16[16,128,576]{1,0,2:T(8,128)(2,1)} %copy.44) | data formatting | bytes 4718592 | tf_op jit(solution)/shard_map/reshape | solution.py:17
  63.4 1.8 copy_bitcast_fusion
  65.2 1.9 all-gather.2.cloned.1.call-done
  67.1 6.1 %fusion.7 = (f32[8,128]{1,0:T(8,128)S(1)}, f32[2048,128,8]{1,0,2:T(8,128)S(1)}) fusion(pred[128,2048]{0,1:T(8,128)(4,1)} %broadcast_compare_fusion, bf16[128,8,576]{0,2,1:T(8,128)(2,1)} %bitcast.92, bf16[2048,576]{0,1:T(8,128)(2,1)} %all-gather.2.cloned.1.call-done), kind=kOutput, calls=%fused_computation.12 | convolution fusion | flops 2422209536 | bytes 12193792 | tf_op jit(solution)/shard_map/thd,pd->htp/dot_general | solution.py:44
  73.2 2.2 select_reduce_fusion
  75.5 1.1 copy-done
  76.5 4.7 %fusion.22 = f32[2048,512]{0,1:T(8,128)} fusion(bf16[128,8,512]{0,2,1:T(8,128)(2,1)S(1)} %bitcast.89, f32[2048,128,8]{1,0,2:T(8,128)S(1)} %get-tuple-element.16, f32[8,128]{1,0:T(8,128)S(1)} %log_add_fusion, pred[128,2048]{0,1:T(8,128)(4,1)S(1)} %copy-done.3), kind=kOutput, calls=%fused_computation.27 | convolution fusion | flops 2157969408 | bytes 13897728 | tf_op jit(solution)/shard_map/htp,the->pe/dot_general | solution.py:77
  81.2 9.9 %multiply_reduce_fusion = (f32[128,8]{0,1:T(8,128)S(1)}, bf16[128,8,512]{2,0,1:T(8,128)(2,1)}) fusion(bf16[128,8,512]{2,0,1:T(8,128)(2,1)} %copy.52, bf16[2048,576]{0,1:T(8,128)(2,1)} %copy_bitcast_fusion, bf16[2048,576,1]{0,1,2:T(8,128)(2,1)S(1)} %copy-done.1, bf16[128,8,576]{0,2,1:T(8,128)(2,1)} %bitcast.93, f32[8,128]{1,0:T(8,128)S(1)} %log_add_fusion, ...), kind=kOutput, calls=%fused_computation.36 | convolution fusion | flops 4576508928 | bytes 8003584 | tf_op jit(solution)/shard_map/htp,pe->the/dot_general | solution.py:62
  91.1 7.2 %fusion.1 = bf16[8,128,2048]{1,2,0:T(8,128)(2,1)S(1)} fusion(f32[2048,128,8]{1,0,2:T(8,128)} %copy-done, bf16[128,8,512]{0,2,1:T(8,128)(2,1)S(1)} %bitcast.90, f32[8,128]{1,0:T(8,128)S(1)} %bitcast.96, f32[8,128]{1,0:T(8,128)S(1)} %log_add_fusion, pred[128,2048]{0,1:T(8,128)(4,1)} %broadcast_compare_fusion, bf16[2048,576]{0,1:T(8,128)(2,1)} %all-gather.2.cloned.1.call-done), kind=kOutput, calls=%fused_computation.2 | convolution fusion | flops 2162163712 | bytes 15998976 | tf_op jit(solution)/shard_map/the,pe->htp/dot_general | solution.py:69
  98.4 2.1 copy-done.6
  100.5 4.3 %fusion.8 = f32[2048,576]{0,1:T(8,128)} fusion(f32[2048,512]{0,1:T(8,128)S(1)} %copy-done.7, bf16[8,128,2048]{1,2,0:T(8,128)(2,1)S(1)} %fusion.1, bf16[128,8,576]{0,2,1:T(8,128)(2,1)S(1)} %bitcast.94), kind=kOutput, calls=%fused_computation.14 | convolution fusion | flops 2418278400 | bytes 14286848 | tf_op jit(solution)/shard_map/htp,thd->pd/dot_general | solution.py:74
  104.7 0.0 reduce-scatter.2.cloned.1.call-update
  104.7 1.2 copy-done.4
  105.9 0.7 copy.48
  106.6 1.3 copy.56
  107.9 5.5 %multiply_convert_fusion = bf16[8,128,576]{1,2,0:T(8,128)(2,1)S(1)} fusion(bf16[8,128,2048]{1,2,0:T(8,128)(2,1)} %copy-done.6, bf16[2048,576]{0,1:T(8,128)(2,1)} %all-gather.2.cloned.1.call-done), kind=kOutput, calls=%fused_computation.33 | convolution fusion | flops 2417098752 | bytes 7733248 | tf_op jit(solution)/shard_map/htp,pd->thd/dot_general | solution.py:73
  113.4 1.4 copy.57
  114.8 59.4 %reduce-scatter.2.cloned.1.call-done = f32[128,576]{0,1:T(8,128)} async-done(((f32[2048,576]{0,1:T(8,128)}), f32[128,576]{0,1:T(8,128)}) %reduce-scatter.2.cloned.1.call-update) | async-done | bytes 294928 | tf_op jit(solution)/shard_map/reduce_scatter | solution.py:84
  174.2 45.8 %all-reduce.2 = bf16[128,576]{0,1:T(8,128)(2,1)} all-reduce(f32[128,576]{0,1:T(8,128)} %reduce-scatter.2.cloned.1.call-done), channel_id=1, replica_groups=mesh['ctx'=16,'head'=8] {'head'}, use_global_device_ids=true, to_apply=%region_6.7 | all-reduce | flops 73728 | bytes 442368 | tf_op jit(solution)/shard_map/psum | solution.py:85
  (19 shorter events, 0.1 us)
Async XLA Ops:
  7.2 60.0 %all-gather.2.cloned.1.call-start = ((), (), s32[]{:S(2)}) async-start(), calls=%async_computation.2 | async-start | bytes 2506752 | tf_op jit(solution)/shard_map/all_gather | solution.py:53
  10.7 44.8 %all-to-all-start = ((bf16[16,128,576]{1,2,0:T(8,128)(2,1)}), bf16[16,128,576]{1,2,0:T(8,128)(2,1)S(1)}, u32[]{:S(2)}, u32[]{:S(2)}) async-start(bf16[16,128,576]{1,2,0:T(8,128)(2,1)} %stack.2), calls=%async_computation | async-start | bytes 4718592 | tf_op jit(solution)/shard_map/all_to_all | solution.py:16
  17.2 5.4 %copy-start.5 = (s32[16]{0:T(128)S(1)}, s32[16]{0:T(128)}, u32[]{:S(2)}) copy-start(s32[16]{0:T(128)} %param.6) | copy-start | bytes 196
  17.2 157.0 %reduce-scatter.2.cloned.1.call-start = ((), (), s32[]{:S(2)}) async-start(), calls=%async_computation.3 | async-start | bytes 5013504 | tf_op jit(solution)/shard_map/reduce_scatter | solution.py:84
  67.1 6.1 %copy-start.3 = (pred[128,2048]{0,1:T(8,128)(4,1)S(1)}, pred[128,2048]{0,1:T(8,128)(4,1)}, u32[]{:S(2)}) copy-start(pred[128,2048]{0,1:T(8,128)(4,1)} %broadcast_compare_fusion) | copy-start | bytes 786436
  73.2 3.3 %copy-start = (f32[2048,128,8]{1,0,2:T(8,128)}, f32[2048,128,8]{1,0,2:T(8,128)S(1)}, u32[]{:S(2)}) copy-start(f32[2048,128,8]{1,0,2:T(8,128)S(1)} %get-tuple-element.16) | copy-start | bytes 25165828
  76.5 4.7 %copy-start.1 = (bf16[2048,576,1]{0,1,2:T(8,128)(2,1)S(1)}, bf16[2048,576,1]{0,1,2:T(8,128)(2,1)}, u32[]{:S(2)}) copy-start(bf16[2048,576,1]{0,1,2:T(8,128)(2,1)} %reshape.128) | copy-start | bytes 7077892
  91.1 9.3 %copy-start.2 = (bf16[128,4608]{0,1:T(8,128)(2,1)S(1)}, bf16[128,4608]{0,1:T(8,128)(2,1)}, u32[]{:S(2)}) copy-start(bf16[128,4608]{0,1:T(8,128)(2,1)} %copy.45) | copy-start | bytes 3538948
  91.1 9.3 %copy-start.7 = (f32[2048,512]{0,1:T(8,128)S(1)}, f32[2048,512]{0,1:T(8,128)}, u32[]{:S(2)}) copy-start(f32[2048,512]{0,1:T(8,128)} %fusion.22) | copy-start | bytes 12582916
  98.4 2.1 copy-start.6
  104.7 1.2 copy-start.4
Sparse Core Ops, SparseCore 0:
  9.6 57.4 all-gather.1
  104.9 69.2 reduce-scatter.1
